TPU v7x, 256 devices: a whole 4x4x8 slice. The times are simulated.
256 devices in a mesh: row: 32 (over x_lo, z, core), col: 8 (over x_hi, y).
Axes of the slice: x: 4 (x_hi: 2, x_lo: 2; x = x_hi * 2 + x_lo), y: 4, z: 8, core: 2. Of those that a mesh axis runs over, the one named last changes fastest.
Arguments:
- ham: bfloat16 [8192, 8192], P('row'), may hold values from -0.2 to 1.7, as said below
- coeff: bfloat16 [8192, 8192], P('row', 'col'), may hold values from -40 to 40, as said below
- tile_mask: int32 [256, 256], P('row'), may hold values from 0 to 1, as said below
- occupation: int32 [16, 8192], replicated, may hold values from 0 to 1, as said below
- orbital_energy: float32 [16], replicated, may hold values from -0.4 to 0.6
- coulomb: float32 [16, 16], replicated, may hold values from 0.005 to 0.04
Outputs:
- correction: float32 [8192, 8192], P('row', 'col')
- stats: float32 [2], replicated
Inputs may be any that keep to these rules, and one draw needn't show every extreme that they name: ham is symmetric. coeff is symmetric. tile_mask is symmetric with ones on its diagonal. `occupation`: every column holds exactly 6 ones.
All inputs are finite; a program needn't handle non-finite values.
Results may differ from a plain program's by a relative error of at most 0.0003.
Values may be sent and summed in bfloat16 or wider, within the bound.
No kernel may reach another device: no remote copies, remote signals or barrier semaphores. Data moves between devices by JAX's collectives and lax.ppermute only.
A program may use at most 128 MiB of HBM per device.

v0:
```python
import jax
import jax.numpy as jnp
from jax import lax
from jax.sharding import PartitionSpec as P

NS = 8192


def turn_tiles(product):
    tile_rows, tile_cols = product.shape
    row_count = lax.axis_size("row")
    col_count = lax.axis_size("col")
    fold_count = row_count // col_count
    sub_rows = tile_rows // row_count
    sectioned = product.reshape(row_count, sub_rows, tile_cols)
    sectioned = lax.all_to_all(
        lax.all_to_all(sectioned, "row", split_axis=0, concat_axis=0, tiled=True),
        "col",
        split_axis=0,
        concat_axis=0,
        tiled=True,
    )
    sectioned = sectioned.reshape(col_count, fold_count, sub_rows, fold_count, tile_rows)
    sectioned = jnp.transpose(sectioned, (0, 3, 1, 2, 4)).reshape(
        row_count, fold_count * sub_rows, tile_rows
    )
    sectioned = lax.all_to_all(sectioned, "row", split_axis=0, concat_axis=0, tiled=True)
    sectioned = sectioned.reshape(row_count, fold_count, sub_rows, tile_rows)
    turned = jnp.transpose(sectioned, (3, 1, 0, 2)).reshape(tile_rows, tile_cols)
    return turned


def body(ham, coeff, tile_mask, occupation, orbital_energy, coulomb):
    tile_rows, strings = ham.shape
    tile_cols = coeff.shape[1]
    mask_cols = tile_mask.shape[1]
    block_size = strings // mask_cols
    mask_rows = tile_rows // block_size
    weights = tile_mask.astype(jnp.bfloat16)[:, None, :, None]
    masked = (ham.reshape(mask_rows, block_size, mask_cols, block_size) * weights).reshape(
        tile_rows, strings
    )
    occ_float = occupation.astype(jnp.float32)
    occ_alpha = lax.dynamic_slice_in_dim(occ_float, lax.axis_index("row") * tile_rows, tile_rows, 1)
    occ_beta = lax.dynamic_slice_in_dim(occ_float, lax.axis_index("col") * tile_cols, tile_cols, 1)
    energy_alpha = jnp.dot(orbital_energy, occ_alpha, precision=lax.Precision.HIGHEST)
    energy_beta = jnp.dot(orbital_energy, occ_beta, precision=lax.Precision.HIGHEST)
    coupling = jnp.dot(
        jnp.dot(occ_alpha.T, coulomb, precision=lax.Precision.HIGHEST),
        occ_beta,
        precision=lax.Precision.HIGHEST,
    )
    diagonal = energy_alpha[:, None] + energy_beta[None, :] + coupling
    product = jnp.dot(
        masked, lax.all_gather(coeff, "row", axis=0, tiled=True), preferred_element_type=jnp.float32
    )
    coeff_float = coeff.astype(jnp.float32)
    sigma = product + turn_tiles(product)
    late = lax.psum(
        (jnp.sum(coeff_float * sigma), jnp.sum(coeff_float * coeff_float)), ("row", "col")
    )
    projection = late[0]
    weight_sum = late[1]
    theta = projection / weight_sum
    residual = sigma - theta * coeff_float
    update = residual / jnp.maximum(jnp.abs(diagonal - theta), 1.0)
    totals = lax.psum((jnp.sum(residual * residual), jnp.sum(update * update)), ("row", "col"))
    correction = update * lax.rsqrt(totals[1] / (NS * NS) + 1e-06)
    stats = jnp.stack([theta, jnp.sqrt(totals[0] / (NS * NS))])
    return (correction, stats)


def solution(mesh):
    in_specs = (P("row", None), P("row", "col"), P("row", None), P(), P(), P())
    out_specs = (P("row", "col"), P())
    return jax.shard_map(body, mesh=mesh, in_specs=in_specs, out_specs=out_specs, check_vma=False)
```

profile of v0, /device:TPU:1, one launch (start us, length us, event | category | flops | bytes accessed | tf_op | source)
XLA Modules:
  0.0 381.5 jit_solution(8685659466072624419)
XLA Ops:
  7.2 0.0 copy-start
  7.2 0.0 all-gather.2.cloned.1.call-start
  7.2 0.7 all-gather.2.cloned.1.call-update
  7.9 0.7 convert_element_type.9
  8.6 6.4 %mul.41 = bf16[8,32,256,32]{3,2,1,0:T(8,128)(2,1)} broadcast(bf16[8,256]{1,0:T(8,128)(2,1)S(1)} %convert_element_type.9), dimensions={0,2} | broadcast | bytes 4198400 | tf_op jit(solution)/shard_map/mul | solution.py:40
  15.0 21.9 %mul.42 = bf16[256,8192]{1,0:T(8,128)(2,1)} reshape(bf16[8,32,256,32]{3,2,1,0:T(8,128)(2,1)} %mul.41) | data formatting | bytes 8388608 | tf_op jit(solution)/shard_map/mul | solution.py:40
  36.9 77.0 %all-gather.2.cloned.1.call-done = bf16[8192,1024]{1,0:T(8,128)(2,1)} async-done(((bf16[256,1024]{1,0:T(8,128)(2,1)}), bf16[8192,1024]{1,0:T(8,128)(2,1)}) %all-gather.2.cloned.1.call-update) | async-done | bytes 16777232 | tf_op jit(solution)/shard_map/all_gather | solution.py:55
  113.9 10.5 %fusion = f32[256,1024]{1,0:T(8,128)S(1)} fusion(bf16[8192,1024]{1,0:T(8,128)(2,1)} %all-gather.2.cloned.1.call-done, bf16[256,8192]{1,0:T(8,128)(2,1)} %param.6, bf16[256,8192]{1,0:T(8,128)(2,1)} %mul.42), kind=kOutput, calls=%fused_computation | convolution fusion | flops 4297064448 | bytes 26214400 | tf_op jit(solution)/shard_map/dot_general | solution.py:54
  124.4 0.0 copy-start.2
  124.4 33.6 %all_to_all.15 = f32[32,8,1024]{2,1,0:T(8,128)S(1)} all-to-all(f32[32,8,1024]{2,1,0:T(8,128)S(1)} %bitcast.25), channel_id=1, replica_groups=mesh['row'=32,'col'=8] {'row'}, dimensions={0} | all-to-all | bytes 2097152 | tf_op jit(solution)/shard_map/all_to_all | solution.py:17
  158.0 0.0 copy-done.2
  158.0 20.1 %all_to_all.16 = f32[32,8,1024]{2,1,0:T(8,128)S(1)} all-to-all(f32[32,8,1024]{2,1,0:T(8,128)S(1)} %all_to_all.15), channel_id=1, replica_groups=mesh['row'=32,'col'=8] {'col'}, dimensions={0} | all-to-all | bytes 2097152 | tf_op jit(solution)/shard_map/all_to_all | solution.py:16
  178.2 0.5 reshape.26
  178.7 1.2 copy.10
  179.8 9.1 %all-to-all-start.2 = ((f32[32,32,256]{2,1,0:T(8,128)}), f32[32,32,256]{2,1,0:T(8,128)S(1)}, u32[]{:S(2)}, u32[]{:S(2)}) async-start(f32[32,32,256]{2,1,0:T(8,128)} %bitcast.2), calls=%async_computation.2 | async-start | bytes 2097152 | tf_op jit(solution)/shard_map/all_to_all | solution.py:27
  188.9 0.0 copy-done.3
  189.0 0.0 copy-done.4
  189.0 0.1 fusion.14
  189.1 0.2 fusion.10
  189.3 0.0 copy-done
  189.3 0.2 fusion.12
  189.5 25.9 %all-to-all-done.2 = f32[32,32,256]{2,1,0:T(8,128)S(1)} async-done(((f32[32,32,256]{2,1,0:T(8,128)}), f32[32,32,256]{2,1,0:T(8,128)S(1)}, u32[]{:S(2)}, u32[]{:S(2)}) %all-to-all-start.2) | async-done | bytes 1048608 | tf_op jit(solution)/shard_map/all_to_all | solution.py:27
  215.4 0.1 copy.11
  215.5 1.3 copy.12
  216.8 0.0 copy-done.1
  216.8 2.6 fusion.7
  219.4 74.3 %all-reduce.1 = (f32[]{:T(128)}, f32[]{:T(128)}) all-reduce(f32[]{:T(128)} %get-tuple-element.3, f32[]{:T(128)} %get-tuple-element.2), channel_id=1, replica_groups=mesh['row'=32,'col'=8] {'row','col'}, use_global_device_ids=true, to_apply=%region_1.0 | all-reduce | flops 2 | bytes 16 | tf_op jit(solution)/shard_map/psum | solution.py:59
  295.1 1.0 multiply_reduce_fusion
  296.0 2.1 multiply_reduce_fusion.1
  298.1 73.5 %all-reduce = (f32[]{:T(128)}, f32[]{:T(128)}) all-reduce(f32[]{:T(128)} %get-tuple-element.9, f32[]{:T(128)} %multiply_reduce_fusion), channel_id=1, replica_groups=mesh['row'=32,'col'=8] {'row','col'}, use_global_device_ids=true, to_apply=%region_5.0 | all-reduce | flops 2 | bytes 16 | tf_op jit(solution)/shard_map/psum | solution.py:67
  373.0 0.6 pad_maximum_fusion
  373.6 1.0 broadcast_multiply_fusion
  (4 shorter events, 0.0 us)
Async XLA Ops:
  7.2 182.1 %copy-start = (f32[16,16]{1,0:T(8,128)S(1)}, f32[16,16]{1,0:T(8,128)}, u32[]{:S(2)}) copy-start(f32[16,16]{1,0:T(8,128)} %param.11) | copy-start | bytes 3076
  7.2 106.7 %all-gather.2.cloned.1.call-start = ((), (), s32[]{:S(2)}) async-start(), calls=%async_computation.3 | async-start | bytes 17301504 | tf_op jit(solution)/shard_map/all_gather | solution.py:55
  124.4 33.6 %copy-start.2 = (f32[256,1024]{1,0:T(8,128)}, f32[256,1024]{1,0:T(8,128)S(1)}, u32[]{:S(2)}) copy-start(f32[256,1024]{1,0:T(8,128)S(1)} %fusion) | copy-start | bytes 3145732
  158.0 30.9 %copy-start.3 = (s32[16,8192]{1,0:T(8,128)S(1)}, s32[16,8192]{1,0:T(8,128)}, u32[]{:S(2)}) copy-start(s32[16,8192]{1,0:T(8,128)} %param.9) | copy-start | bytes 1572868
  178.2 10.8 %copy-start.4 = (f32[16]{0:T(128)S(1)}, f32[16]{0:T(128)}, u32[]{:S(2)}) copy-start(f32[16]{0:T(128)} %param.10) | copy-start | bytes 196
  179.8 37.0 %copy-start.1 = (bf16[256,1024]{1,0:T(8,128)(2,1)S(1)}, bf16[256,1024]{1,0:T(8,128)(2,1)}, u32[]{:S(2)}) copy-start(bf16[256,1024]{1,0:T(8,128)(2,1)} %param.7) | copy-start | bytes 1572868
  179.8 35.5 %all-to-all-start.2 = ((f32[32,32,256]{2,1,0:T(8,128)}), f32[32,32,256]{2,1,0:T(8,128)S(1)}, u32[]{:S(2)}, u32[]{:S(2)}) async-start(f32[32,32,256]{2,1,0:T(8,128)} %bitcast.2), calls=%async_computation.2 | async-start | bytes 2097152 | tf_op jit(solution)/shard_map/all_to_all | solution.py:27
Sparse Core Ops, SparseCore 0:
  9.9 103.9 all-gather.1
where the time goes:
time: 382 us; the launch traced here: 381 us
  blocking collectives  202 us (53%)
  waiting for transfers between devices  104 us (27%)
  local copies, waits for them, and re-layouts  31.4 us (8%)
  between operations  16.9 us (4%)
  matrix products  13.1 us (3%)
  starting transfers between devices  9.11 us (2%)
  other arithmetic  5.93 us (2%)
    all_gather x1, waiting for transfers between devices, body(): lax.all_gather(coeff, 'row', axis=0, tiled=True)  77 us
    psum x1, blocking collectives, body(): lax.psum((jnp.sum(coeff_float * sigma), jnp.sum(coeff_float * coeff_float...  74.3 us
    psum x1, blocking collectives, body(): lax.psum((jnp.sum(residual * residual), jnp.sum(update * update)), ('row'...  73.5 us
    all_to_all x1, blocking collectives, turn_tiles(): lax.all_to_all(sectioned, 'row', split_axis=0, concat_axis=0, tiled=True)  33.6 us
    mul x2, local copies, waits for them, and re-layouts, body(): ham.reshape(mask_rows, block_size, mask_cols, block_size) * weights  28.3 us
    all_to_all x1, waiting for transfers between devices, turn_tiles(): lax.all_to_all(sectioned, 'row', split_axis=0, concat_axis=0, tiled=True)  25.9 us
    all_to_all x1, blocking collectives, turn_tiles(): lax.all_to_all(lax.all_to_all(sectioned, 'row', split_axis=0, concat_axis...  20.1 us
    dot_general x1, matrix products, body(): jnp.dot(masked, lax.all_gather(coeff, 'row', axis=0, tiled=True), preferr...  10.5 us
  transfers between devices with their start and end apart: 2, of which 2 were waited for; matrix products, arithmetic and copies ran while one was open for 8% of the time, Pallas kernels for 0%

commit v1 on v0

--- a/solution.py
+++ b/solution.py
@@ -4,6 +4,13 @@
 from jax.sharding import PartitionSpec as P
 
 NS = 8192
+
+
+def exchange_gather(x, mesh_axis, dim):
+    n_dev = lax.axis_size(mesh_axis)
+    parts = jnp.stack([x for _ in range(n_dev)])
+    parts = lax.all_to_all(parts, mesh_axis, split_axis=0, concat_axis=0)
+    return jnp.concatenate(parts, axis=dim)
 
 
 def turn_tiles(product):
@@ -51,9 +58,7 @@
         precision=lax.Precision.HIGHEST,
     )
     diagonal = energy_alpha[:, None] + energy_beta[None, :] + coupling
-    product = jnp.dot(
-        masked, lax.all_gather(coeff, "row", axis=0, tiled=True), preferred_element_type=jnp.float32
-    )
+    product = jnp.dot(masked, exchange_gather(coeff, "row", 0), preferred_element_type=jnp.float32)
     coeff_float = coeff.astype(jnp.float32)
     sigma = product + turn_tiles(product)
     late = lax.psum(

time: 382 us -> 652 us (1.71)
  waiting for transfers between devices: 104 us -> 359 us
  between operations: 16.9 us -> 3.52 us
  starting transfers between devices: 9.11 us -> 20.3 us
  blocking collectives: 202 us -> 212 us
  local copies, waits for them, and re-layouts: 31.4 us -> 38 us
    all_to_all x0 -> x1, waiting for transfers between devices: none -> 333 us  [exchange_gather(): parts = lax.all_to_all(parts, mesh_axis, split_axis=0, concat_axis=0)]
    all_gather x1 -> x0, waiting for transfers between devices: 77 us -> none  [body(): lax.all_gather(coeff, 'row', axis=0, tiled=True)]
    all_to_all x0 -> x1, starting transfers between devices: none -> 11.2 us  [exchange_gather(): parts = lax.all_to_all(parts, mesh_axis, split_axis=0, concat_axis=0)]
    all_to_all x1, blocking collectives: 33.6 us -> 43.9 us  [turn_tiles(): lax.all_to_all(sectioned, 'row', split_axis=0, concat_axis=0, tiled=True)]
    another operation x0 -> x1, local copies, waits for them, and re-layouts: none -> 6.81 us  [exchange_gather(): parts = jnp.stack([x for _ in range(n_dev)])]
  transfers between devices with their start and end apart: 2 -> 2, of which waited for: 2 -> 2; matrix products, arithmetic and copies ran while one was open for 8% -> 4% of each run, Pallas kernels for 0% -> 0%
where the time goes in v1:
time: 652 us; the launch traced here: 651 us
  waiting for transfers between devices  359 us (55%)
  blocking collectives  212 us (33%)
  local copies, waits for them, and re-layouts  38 us (6%)
  starting transfers between devices  20.3 us (3%)
  matrix products  13.1 us (2%)
    all_to_all x1, waiting for transfers between devices, exchange_gather(): parts = lax.all_to_all(parts, mesh_axis, split_axis=0, concat_axis=0)  333 us
    psum x1, blocking collectives, body(): lax.psum((jnp.sum(coeff_float * sigma), jnp.sum(coeff_float * coeff_float...  74.3 us
    psum x1, blocking collectives, body(): lax.psum((jnp.sum(residual * residual), jnp.sum(update * update)), ('row'...  73.5 us
    all_to_all x1, blocking collectives, turn_tiles(): lax.all_to_all(sectioned, 'row', split_axis=0, concat_axis=0, tiled=True)  43.9 us
    mul x2, local copies, waits for them, and re-layouts, body(): ham.reshape(mask_rows, block_size, mask_cols, block_size) * weights  28.1 us
    all_to_all x1, waiting for transfers between devices, turn_tiles(): lax.all_to_all(sectioned, 'row', split_axis=0, concat_axis=0, tiled=True)  25.9 us
    all_to_all x1, blocking collectives, turn_tiles(): lax.all_to_all(lax.all_to_all(sectioned, 'row', split_axis=0, concat_axis...  20.4 us
  transfers between devices with their start and end apart: 2, of which 2 were waited for; matrix products, arithmetic and copies ran while one was open for 4% of the time, Pallas kernels for 0%

profile of v1, /device:TPU:1, one launch (start us, length us, event | category | flops | bytes accessed | tf_op | source)
XLA Modules:
  0.0 651.0 jit_solution(2966094266446759296)
XLA Ops:
  0.6 0.0 copy-start
  0.6 6.8 %stack.8 = bf16[32,256,1024]{2,1,0:T(8,128)(2,1)} broadcast(bf16[256,1024]{1,0:T(8,128)(2,1)} %param.7), dimensions={1,2} | broadcast | bytes 17301504 | tf_op jit(solution)/shard_map/stack | solution.py:11
  7.5 11.2 %all-to-all-start = ((bf16[32,256,1024]{2,1,0:T(8,128)(2,1)}), bf16[32,256,1024]{2,1,0:T(8,128)(2,1)}, u32[]{:S(2)}, u32[]{:S(2)}) async-start(bf16[32,256,1024]{2,1,0:T(8,128)(2,1)} %stack.8), calls=%async_computation | async-start | bytes 33554432 | tf_op jit(solution)/shard_map/all_to_all | solution.py:12
  18.7 0.0 copy-done.4
  18.7 6.4 mul.41
  25.1 21.7 %mul.42 = bf16[256,8192]{1,0:T(8,128)(2,1)} reshape(bf16[8,32,256,32]{3,2,1,0:T(8,128)(2,1)} %mul.41) | data formatting | bytes 8388608 | tf_op jit(solution)/shard_map/mul | solution.py:47
  46.8 333.0 %all-to-all-done = bf16[32,256,1024]{2,1,0:T(8,128)(2,1)} async-done(((bf16[32,256,1024]{2,1,0:T(8,128)(2,1)}), bf16[32,256,1024]{2,1,0:T(8,128)(2,1)}, u32[]{:S(2)}, u32[]{:S(2)}) %all-to-all-start) | async-done | bytes 16777248 | tf_op jit(solution)/shard_map/all_to_all | solution.py:12
  379.8 10.5 %fusion = f32[256,1024]{1,0:T(8,128)S(1)} fusion(bf16[8192,1024]{1,0:T(8,128)(2,1)} %bitcast, bf16[256,8192]{1,0:T(8,128)(2,1)} %param.6, bf16[256,8192]{1,0:T(8,128)(2,1)} %mul.42), kind=kOutput, calls=%fused_computation | convolution fusion | flops 4297064448 | bytes 26214400 | tf_op jit(solution)/shard_map/dot_general | solution.py:61
  390.3 0.0 copy-start.2
  390.3 43.9 %all_to_all.20 = f32[32,8,1024]{2,1,0:T(8,128)S(1)} all-to-all(f32[32,8,1024]{2,1,0:T(8,128)S(1)} %bitcast.26), channel_id=1, replica_groups=mesh['row'=32,'col'=8] {'row'}, dimensions={0} | all-to-all | bytes 2097152 | tf_op jit(solution)/shard_map/all_to_all | solution.py:24
  434.2 0.0 copy-done.2
  434.2 20.4 %all_to_all.21 = f32[32,8,1024]{2,1,0:T(8,128)S(1)} all-to-all(f32[32,8,1024]{2,1,0:T(8,128)S(1)} %all_to_all.20), channel_id=1, replica_groups=mesh['row'=32,'col'=8] {'col'}, dimensions={0} | all-to-all | bytes 2097152 | tf_op jit(solution)/shard_map/all_to_all | solution.py:23
  454.5 0.5 reshape.32
  455.0 1.2 copy.10
  456.2 9.1 %all-to-all-start.3 = ((f32[32,32,256]{2,1,0:T(8,128)}), f32[32,32,256]{2,1,0:T(8,128)S(1)}, u32[]{:S(2)}, u32[]{:S(2)}) async-start(f32[32,32,256]{2,1,0:T(8,128)} %bitcast.3), calls=%async_computation.3 | async-start | bytes 2097152 | tf_op jit(solution)/shard_map/all_to_all | solution.py:34
  465.3 0.0 copy-done.3
  465.4 0.0 copy-done.5
  465.4 0.1 fusion.14
  465.5 0.2 fusion.10
  465.7 0.0 copy-done
  465.7 0.2 fusion.12
  465.9 25.9 %all-to-all-done.3 = f32[32,32,256]{2,1,0:T(8,128)S(1)} async-done(((f32[32,32,256]{2,1,0:T(8,128)}), f32[32,32,256]{2,1,0:T(8,128)S(1)}, u32[]{:S(2)}, u32[]{:S(2)}) %all-to-all-start.3) | async-done | bytes 1048608 | tf_op jit(solution)/shard_map/all_to_all | solution.py:34
  491.8 0.1 copy.11
  491.9 1.3 copy.12
  493.2 0.0 copy-done.1
  493.2 2.6 fusion.7
  495.8 74.3 %all-reduce.1 = (f32[]{:T(128)}, f32[]{:T(128)}) all-reduce(f32[]{:T(128)} %get-tuple-element.3, f32[]{:T(128)} %get-tuple-element.2), channel_id=1, replica_groups=mesh['row'=32,'col'=8] {'row','col'}, use_global_device_ids=true, to_apply=%region_1.0 | all-reduce | flops 2 | bytes 16 | tf_op jit(solution)/shard_map/psum | solution.py:64
  571.4 1.0 multiply_reduce_fusion
  572.4 2.1 multiply_reduce_fusion.1
  574.5 73.5 %all-reduce = (f32[]{:T(128)}, f32[]{:T(128)}) all-reduce(f32[]{:T(128)} %get-tuple-element.9, f32[]{:T(128)} %multiply_reduce_fusion), channel_id=1, replica_groups=mesh['row'=32,'col'=8] {'row','col'}, use_global_device_ids=true, to_apply=%region_5.0 | all-reduce | flops 2 | bytes 16 | tf_op jit(solution)/shard_map/psum | solution.py:72
  649.4 0.6 pad_maximum_fusion
  649.9 1.0 broadcast_multiply_fusion
  (6 shorter events, 0.0 us)
Async XLA Ops:
  0.6 465.1 %copy-start = (f32[16,16]{1,0:T(8,128)S(1)}, f32[16,16]{1,0:T(8,128)}, u32[]{:S(2)}) copy-start(f32[16,16]{1,0:T(8,128)} %param.11) | copy-start | bytes 3076
  7.5 11.3 %copy-start.4 = (s32[8,256]{1,0:T(8,128)S(1)}, s32[8,256]{1,0:T(8,128)}, u32[]{:S(2)}) copy-start(s32[8,256]{1,0:T(8,128)} %param.8) | copy-start | bytes 24580
  7.5 372.3 %all-to-all-start = ((bf16[32,256,1024]{2,1,0:T(8,128)(2,1)}), bf16[32,256,1024]{2,1,0:T(8,128)(2,1)}, u32[]{:S(2)}, u32[]{:S(2)}) async-start(bf16[32,256,1024]{2,1,0:T(8,128)(2,1)} %stack.8), calls=%async_computation | async-start | bytes 33554432 | tf_op jit(solution)/shard_map/all_to_all | solution.py:12
  390.3 43.9 %copy-start.2 = (f32[256,1024]{1,0:T(8,128)}, f32[256,1024]{1,0:T(8,128)S(1)}, u32[]{:S(2)}) copy-start(f32[256,1024]{1,0:T(8,128)S(1)} %fusion) | copy-start | bytes 3145732
  434.2 31.1 %copy-start.3 = (s32[16,8192]{1,0:T(8,128)S(1)}, s32[16,8192]{1,0:T(8,128)}, u32[]{:S(2)}) copy-start(s32[16,8192]{1,0:T(8,128)} %param.9) | copy-start | bytes 1572868
  454.5 10.8 %copy-start.5 = (f32[16]{0:T(128)S(1)}, f32[16]{0:T(128)}, u32[]{:S(2)}) copy-start(f32[16]{0:T(128)} %param.10) | copy-start | bytes 196
  456.2 37.0 %copy-start.1 = (bf16[256,1024]{1,0:T(8,128)(2,1)S(1)}, bf16[256,1024]{1,0:T(8,128)(2,1)}, u32[]{:S(2)}) copy-start(bf16[256,1024]{1,0:T(8,128)(2,1)} %param.7) | copy-start | bytes 1572868
  456.2 35.5 %all-to-all-start.3 = ((f32[32,32,256]{2,1,0:T(8,128)}), f32[32,32,256]{2,1,0:T(8,128)S(1)}, u32[]{:S(2)}, u32[]{:S(2)}) async-start(f32[32,32,256]{2,1,0:T(8,128)} %bitcast.3), calls=%async_computation.3 | async-start | bytes 2097152 | tf_op jit(solution)/shard_map/all_to_all | solution.py:34
